TPU v7x, 32 devices: a whole 2x2x4 slice. The times are simulated.
32 devices in a mesh: mem: 8 (over z, x), pb: 4 (over y, core).
Axes of the slice: x: 2, y: 2, z: 4, core: 2. Of those that a mesh axis runs over, the one named last changes fastest.
Arguments:
- queries: bfloat16 [4096, 1024], P(('pb', 'mem')), may hold values from -9 to 9
- local_keys: bfloat16 [4096, 1024], P(('pb', 'mem')), may hold values from -9 to 9
- local_values: bfloat16 [4096, 1024], P(('pb', 'mem')), may hold values from -6 to 6
- memory_keys: bfloat16 [8192, 1024], P('mem'), may hold values from -11 to 11
- memory_values: bfloat16 [8192, 1024], P('mem'), may hold values from -6 to 6
- neighbour_index_rows: int32 [4096, 32], P(('pb', 'mem')), may hold values from 0 to 8191, as said below
- gate_bias: float32 [8], replicated, may hold values from -2.5 to 2.5
- out_weight: bfloat16 [1024, 1024], P('pb'), may hold values from -0.75 to 0.75
Outputs:
- layer_out: bfloat16 [4096, 1024], P(('pb', 'mem'))
Inputs may be any that keep to these rules, and one draw needn't show every extreme that they name: `neighbour_index_rows`: memory shard o holds rows o * 1024 to (o + 1) * 1024 - 1. Among the 4096 ids of one device's rows, at most 1024 fall in any one shard, and exactly 1024 fall in some shard; for each index of pb, one shard receives exactly 1024 from every device with that index. Ids of a row may repeat.
All inputs are finite; a program needn't handle non-finite values.
Results may differ from a plain program's by a relative error of at most 0.01.
Values may be sent and summed in bfloat16 or wider, within the bound.
A program may use at most 192 MiB of HBM per device.

v0:
```python
import math

import jax
import jax.numpy as jnp
from jax import lax
from jax.sharding import PartitionSpec as P


def combined_all(value, axis, join):
    pieces = jax.tree.map(lambda part: lax.all_gather(part, axis), value)
    head = jax.tree.map(lambda part: part[0], pieces)
    tail = jax.tree.map(lambda part: part[1:], pieces)
    subtotal, _ = lax.scan(lambda subtotal, share: (join(subtotal, share), None), head, tail)
    return subtotal


def join_totals(first, second):
    peak = jnp.maximum(first[0], second[0])
    return (peak, first[1] * jnp.exp(first[0] - peak) + second[1] * jnp.exp(second[0] - peak))


def slot_ranks(owners, count):
    onehot = (owners[:, None] == jnp.arange(count, dtype=jnp.int32)[None, :]).astype(jnp.int32)
    return jnp.sum(jnp.cumsum(onehot, axis=0) * onehot, axis=1) - 1


def body(
    queries,
    local_keys,
    local_values,
    memory_keys,
    memory_values,
    neighbour_index_rows,
    gate_bias,
    out_weight,
):
    shard_count = lax.axis_size("mem")
    my_shard = lax.axis_index("mem")
    row_count = queries.shape[0]
    model_width = queries.shape[1]
    head_count = gate_bias.shape[0]
    head_size = model_width // head_count
    memory_rows = memory_keys.shape[0]
    top_count = neighbour_index_rows.shape[1]
    capacity = 2 * row_count * top_count // shard_count
    group_rows = shard_count * row_count
    multiplier = head_size ** (-0.5)
    row_numbers = jnp.arange(row_count, dtype=jnp.int32)
    group_queries = lax.all_gather(queries, "mem", axis=0, tiled=True)
    query_heads = queries.reshape(row_count, head_count, head_size)
    key_local = local_keys.reshape(row_count, head_count, head_size)
    value_local = local_values.reshape(row_count, head_count, head_size)
    local_scores = (
        jnp.einsum("qhd,khd->hqk", query_heads, key_local, preferred_element_type=jnp.float32)
        * multiplier
    )
    causal = row_numbers[:, None] >= row_numbers[None, :]
    local_scores = jnp.where(causal[None], local_scores, -jnp.inf)
    local_peak = jnp.max(local_scores, axis=-1, keepdims=True)
    local_expo = jnp.exp(local_scores - local_peak)
    local_weights = (local_expo / jnp.sum(local_expo, axis=-1, keepdims=True)).astype(jnp.bfloat16)
    local_out = jnp.einsum(
        "hqk,khd->qhd", local_weights, value_local, preferred_element_type=jnp.float32
    )
    key_head_count = memory_keys.reshape(memory_rows, head_count, head_size)
    block = math.gcd(group_rows, 512)

    def block_stats(query_tile_block):
        reshaped_tensor = query_tile_block.reshape(block, head_count, head_size)
        logit_scores = (
            jnp.einsum(
                "bvt,yvt->bvy", reshaped_tensor, key_head_count, preferred_element_type=jnp.float32
            )
            * multiplier
        )
        block_peak = jnp.max(logit_scores, axis=2)
        return (block_peak, jnp.sum(jnp.exp(logit_scores - block_peak[:, :, None]), axis=2))

    peaks, totals = lax.map(
        block_stats, group_queries.reshape(group_rows // block, block, model_width)
    )
    peaks = peaks.reshape(group_rows, head_count)
    totals = totals.reshape(group_rows, head_count)
    global_peak, global_total = combined_all((peaks, totals), "mem", join_totals)
    source_queries = group_queries.reshape(shard_count, row_count, head_count, head_size)
    source_peaks = global_peak.reshape(shard_count, row_count, head_count)
    flat_ids = neighbour_index_rows.reshape(-1)
    entry_row_list = jnp.arange(row_count * top_count, dtype=jnp.int32) // top_count
    owners = flat_ids // memory_rows
    ranks = slot_ranks(owners, shard_count)
    codes = entry_row_list * memory_rows + flat_ids % memory_rows
    slots = owners * capacity + ranks
    requests = (
        jnp.full((shard_count * capacity,), -1, jnp.int32)
        .at[slots]
        .set(codes)
        .reshape(shard_count, capacity)
    )
    slot_owner_row = (
        jnp.full((shard_count * capacity,), -1, jnp.int32).at[slots].set(entry_row_list)
    )
    codes = lax.all_to_all(requests, "mem", split_axis=0, concat_axis=0, tiled=True)
    valid = codes >= 0
    safe = jnp.where(valid, codes, 0)
    offsets = safe % memory_rows
    local_rows = jnp.where(valid, safe // memory_rows, -1)
    slot_width = codes.shape[1]
    picked_keys = memory_keys[offsets].reshape(codes.shape[0], slot_width, head_count, head_size)
    values = memory_values[offsets]

    def score_source(inputs):
        query_block, key_block, rows_here, peak_block = inputs
        full = (
            jnp.einsum("qhd,chd->hqc", query_block, key_block, preferred_element_type=jnp.float32)
            * multiplier
        )
        hit = rows_here[None, :] == row_numbers[:, None]
        scores = jnp.sum(jnp.where(hit[None], full, 0.0), axis=1)
        peak_here = jnp.sum(jnp.where(hit[:, :, None], peak_block[:, None, :], 0.0), axis=0)
        weight_here = jnp.exp(scores.T - peak_here)
        return jnp.where((rows_here >= 0)[:, None], weight_here, 0.0).astype(jnp.bfloat16)

    weights = lax.map(score_source, (source_queries, picked_keys, local_rows, source_peaks))
    weights, values, local_rows = (weights, values, local_rows)
    values, weights = (
        lax.all_to_all(values, "mem", split_axis=0, concat_axis=0, tiled=True),
        lax.all_to_all(weights, "mem", split_axis=0, concat_axis=0, tiled=True),
    )
    flat_values = values.reshape(shard_count * capacity, head_count, head_size)
    flat_weights = weights.reshape(shard_count * capacity, head_count)
    hit = slot_owner_row[None, :] == row_numbers[:, None]
    scaled = jnp.where(hit[None], flat_weights.T[:, None, :], jnp.zeros((), jnp.bfloat16))
    numerator = jnp.einsum("hqs,shd->qhd", scaled, flat_values, preferred_element_type=jnp.float32)
    denominator = jnp.dot(
        hit.astype(jnp.bfloat16), flat_weights, preferred_element_type=jnp.float32
    )
    own_total = lax.dynamic_slice_in_dim(global_total, my_shard * row_count, row_count, 0)
    background = top_count / (memory_rows * shard_count) * own_total
    memory_out = numerator / (denominator + background)[:, :, None]
    gate = jax.nn.sigmoid(gate_bias)[None, :, None]
    mixed = (
        (gate * memory_out + (1.0 - gate) * local_out)
        .reshape(row_count, model_width)
        .astype(jnp.bfloat16)
    )
    result = jnp.dot(
        mixed,
        lax.all_gather(out_weight, "pb", axis=0, tiled=True),
        preferred_element_type=jnp.float32,
    )
    return result.astype(jnp.bfloat16)


def solution(mesh):
    in_specs = (
        P(("pb", "mem"), None),
        P(("pb", "mem"), None),
        P(("pb", "mem"), None),
        P("mem", None),
        P("mem", None),
        P(("pb", "mem"), None),
        P(),
        P("pb", None),
    )
    out_specs = P(("pb", "mem"), None)
    return jax.shard_map(body, mesh=mesh, in_specs=in_specs, out_specs=out_specs, check_vma=False)
```

profile of v0, /device:TPU:0, one launch (start us, length us, event | category | flops | bytes accessed | tf_op | source)
XLA Modules:
  0.0 718.5 jit_solution(11344651262773590090)
XLA Ops:
  12.4 16.1 %scatter_custom_fusion = s32[8192]{0:T(1024)} fusion(s32[4096]{0:T(1024)S(1)} %bitcast.179, s32[4096]{0:T(1024)S(1)} %get-tuple-element.207, s32[]{:T(128)} %constant.123.clone.1), kind=kCustom, calls=%fused_computation.112 | custom fusion | bytes 32772 | tf_op jit(solution)/shard_map/scatter | solution.py:96
  28.5 7.3 %all-to-all-start = ((s32[8,1,1024]{2,1,0:T(1,128)}), s32[8,1,1024]{2,1,0:T(1,128)S(1)}, u32[]{:S(2)}, u32[]{:S(2)}) async-start(s32[8,1,1024]{2,1,0:T(1,128)} %bitcast.9), calls=%async_computation | async-start | bytes 65536 | tf_op jit(solution)/shard_map/all_to_all | solution.py:102
  35.8 4.0 copy.67
  39.7 3.9 copy.69
  43.8 42.5 %gather_fusion.1 = bf16[8192,1024]{1,0:T(8,128)(2,1)} fusion(bf16[1024,1024]{1,0:T(8,128)(2,1)} %param.17, s32[8192]{0:T(1024)S(1)} %broadcast_clamp_fusion), kind=kCustom, calls=%fused_computation.1 | custom fusion | bytes 33587200 | tf_op jit(solution)/shard_map/gather | solution.py:108
  86.3 15.6 %copy.87 = bf16[1024,8,8,128]{3,2,1,0:T(8,128)(2,1)} copy(bf16[1024,8,8,128]{3,1,2,0:T(8,128)(2,1)} %bitcast.161) | data formatting | bytes 33554432
  102.0 23.2 %while.35 = (s32[]{:T(128)}, f32[2,512,8]{1,2,0:T(8,128)S(1)}, f32[2,512,8]{1,2,0:T(8,128)S(1)}, bf16[2,512,1024]{2,1,0:T(8,128)(2,1)}, bf16[1024,8,128]{2,0,1:T(8,128)(2,1)}, /*index=5*/s32[]{:T(128)}) while((s32[]{:T(128)}, f32[2,512,8]{1,2,0:T(8,128)S(1)}, f32[2,512,8]{1,2,0:T(8,128)S(1)}, bf16[2,512,1024]{2,1,0:T(8,128)(2,1)}, ...), condition=%wide.region_8.9_spmd, body=%wide.region_5.8_spmd.sunk | while | flops 1094705152 | bytes 41009228 | solution.py:79
  105.8 4.2 bitcast_reduce_fusion.2
  110.1 3.5 fusion.76
  117.4 4.2 bitcast_reduce_fusion.2
  121.6 3.5 fusion.76
  125.2 31.4 %all_gather.14 = f32[8,1024,8]{1,2,0:T(8,128)S(1)} all-gather(f32[1,1024,8]{1,2,0:T(8,128)S(1)} %bitcast.177), channel_id=1, replica_groups=mesh['mem'=8,'pb'=4] {'mem'}, dimensions={0}, use_global_device_ids=true | all-gather | bytes 294912 | tf_op jit(solution)/shard_map/all_gather | solution.py:10
  156.6 30.7 %all_gather.13 = f32[8,1024,8]{1,2,0:T(8,128)S(1)} all-gather(f32[1,1024,8]{1,2,0:T(8,128)S(1)} %bitcast.176), channel_id=1, replica_groups=mesh['mem'=8,'pb'=4] {'mem'}, dimensions={0}, use_global_device_ids=true | all-gather | bytes 294912 | tf_op jit(solution)/shard_map/all_gather | solution.py:10
  187.8 3.6 copy.86
  191.4 43.2 %while.37 = (s32[]{:T(128)}, bf16[8,1024,8]{1,2,0:T(8,128)(2,1)}, s32[8,1024]{1,0:T(8,128)S(1)}, bf16[8,128,8,128]{3,2,1,0:T(8,128)(2,1)}, bf16[8,1024,8,128]{3,...) while((s32[]{:T(128)}, bf16[8,1024,8]{1,2,0:T(8,128)(2,1)}, ...), condition=%wide.region_14.15_spmd.clone, body=%wide.region_11.14_spmd.clone.sunk | while | flops 273818624 | bytes 7658077 | solution.py:123
  234.6 5.4 all-to-all-start.2
  239.9 35.4 %gather_fusion = bf16[8192,1024]{1,0:T(8,128)(2,1)} fusion(bf16[1024,1024]{1,0:T(8,128)(2,1)S(1)} %copy-done, s32[8192]{0:T(1024)S(1)} %broadcast_clamp_fusion), kind=kCustom, calls=%fused_computation | custom fusion | bytes 33587200 | tf_op jit(solution)/shard_map/gather | solution.py:109
  275.4 21.6 %copy.65 = bf16[8,1024,1024]{1,2,0:T(8,128)(2,1)} copy(bf16[8,1024,1024]{2,1,0:T(8,128)(2,1)} %bitcast.160) | data formatting | bytes 33554432 | tf_op jit(solution)/shard_map/gather | solution.py:109
  297.0 6.1 all-to-all-start.1
  303.7 15.7 %scatter_custom_fusion.1 = s32[8192]{0:T(1024)S(1)} fusion(s32[4096]{0:T(1024)} %bitcast.180, s32[4096]{0:T(1024)S(1)} %add_select_fusion.2, s32[]{:T(128)} %constant.123.clone.1), kind=kCustom, calls=%fused_computation.110 | custom fusion | bytes 33280 | tf_op jit(solution)/shard_map/scatter | solution.py:100
  322.1 331.0 %all-to-all-done.1 = bf16[8,1024,1024]{1,2,0:T(8,128)(2,1)} async-done(((bf16[8,1024,1024]{1,2,0:T(8,128)(2,1)}), bf16[8,1024,1024]{1,2,0:T(8,128)(2,1)}, u32[]{:S(2)}, u32[]{:S(2)}) %all-to-all-start.1) | async-done | bytes 16777248 | tf_op jit(solution)/shard_map/all_to_all | solution.py:126
  653.1 18.7 %copy.66 = bf16[8,1024,1024]{1,0,2:T(8,128)(2,1)} copy(bf16[8,1024,1024]{1,2,0:T(8,128)(2,1)} %all-to-all-done.1) | data formatting | bytes 33554432 | tf_op jit(solution)/shard_map/all_to_all | solution.py:126
  671.8 25.6 %reshape.338 = bf16[8192,8,128]{0,2,1:T(8,128)(2,1)} reshape(bf16[8,1024,1024]{1,0,2:T(8,128)(2,1)} %copy.66) | data formatting | bytes 33554432 | tf_op jit(solution)/shard_map/reshape | solution.py:129
  697.4 9.2 %fusion.29 = f32[128,8,128]{0,2,1:T(8,128)} fusion(bf16[8192,8,128]{0,2,1:T(8,128)(2,1)} %reshape.338, pred[128,8192]{1,0:T(8,128)(4,1)S(1)} %iota_compare_fusion.1, bf16[8,8192]{1,0:T(8,128)(2,1)S(1)} %bitcast.173, f32[128,8]{0,1:T(8,128)S(1)} %convolution_add_fusion, f32[8]{0:T(128)S(1)} %get-tuple-element.202), kind=kOutput, calls=%fused_computation.52 | convolution fusion | flops 2156134400 | bytes 18485280 | tf_op jit(solution)/shard_map/hqs,shd->qhd/dot_general | solution.py:133
  (152 shorter events, 64.0 us)
Async XLA Ops:
  7.4 232.6 %copy-start = (bf16[1024,1024]{1,0:T(8,128)(2,1)S(1)}, bf16[1024,1024]{1,0:T(8,128)(2,1)}, u32[]{:S(2)}) copy-start(bf16[1024,1024]{1,0:T(8,128)(2,1)} %param.18) | copy-start | bytes 6291460
  7.4 94.7 %all-gather.3.cloned.1.call-start = ((), (), s32[]{:S(2)}) async-start(), calls=%async_computation.3 | async-start | bytes 2359296 | tf_op jit(solution)/shard_map/all_gather | solution.py:49
  12.4 31.3 %copy-start.5 = (s32[4096,1]{0,1:T(1,128)}, s32[4096,1]{0,1:T(1,128)S(1)}, u32[]{:S(2)}) copy-start(s32[4096,1]{0,1:T(1,128)S(1)} %compare_select_fusion.4) | copy-start | bytes 49156
  28.5 15.2 %all-to-all-start = ((s32[8,1,1024]{2,1,0:T(1,128)}), s32[8,1,1024]{2,1,0:T(1,128)S(1)}, u32[]{:S(2)}, u32[]{:S(2)}) async-start(s32[8,1,1024]{2,1,0:T(1,128)} %bitcast.9), calls=%async_computation | async-start | bytes 65536 | tf_op jit(solution)/shard_map/all_to_all | solution.py:102
  234.6 62.4 %all-to-all-start.2 = ((bf16[8,1024,8]{1,2,0:T(8,128)(2,1)}), bf16[8,1024,8]{1,2,0:T(8,128)(2,1)S(1)}, u32[]{:S(2)}, u32[]{:S(2)}) async-start(bf16[8,1024,8]{1,2,0:T(8,128)(2,1)} %get-tuple-element.101), calls=%async_computation.2 | async-start | bytes 262144 | tf_op jit(solution)/shard_map/all_to_all | solution.py:127
  296.9 22.5 %copy-start.3 = (bf16[128,1024]{1,0:T(8,128)(2,1)S(1)}, bf16[128,1024]{1,0:T(8,128)(2,1)}, u32[]{:S(2)}) copy-start(bf16[128,1024]{1,0:T(8,128)(2,1)} %param.16) | copy-start | bytes 786436
  296.9 23.3 %copy-start.4 = (bf16[128,1024]{1,0:T(8,128)(2,1)S(1)}, bf16[128,1024]{1,0:T(8,128)(2,1)}, u32[]{:S(2)}) copy-start(bf16[128,1024]{1,0:T(8,128)(2,1)} %param.14) | copy-start | bytes 786436
  296.9 23.3 %copy-start.6 = (bf16[128,1024]{1,0:T(8,128)(2,1)S(1)}, bf16[128,1024]{1,0:T(8,128)(2,1)}, u32[]{:S(2)}) copy-start(bf16[128,1024]{1,0:T(8,128)(2,1)} %param.15) | copy-start | bytes 786436
  296.9 23.8 %copy-start.7 = (f32[8]{0:T(128)S(1)}, f32[8]{0:T(128)}, u32[]{:S(2)}) copy-start(f32[8]{0:T(128)} %param.20) | copy-start | bytes 100
  297.0 356.1 %all-to-all-start.1 = ((bf16[8,1024,1024]{1,2,0:T(8,128)(2,1)}), bf16[8,1024,1024]{1,2,0:T(8,128)(2,1)}, u32[]{:S(2)}, u32[]{:S(2)}) async-start(bf16[8,1024,1024]{1,2,0:T(8,128)(2,1)} %copy.65), calls=%async_computation.1 | async-start | bytes 33554432 | tf_op jit(solution)/shard_map/all_to_all | solution.py:126
  303.1 405.2 %all-gather.5.cloned.1.call-start = ((), (), s32[]{:S(2)}) async-start(), calls=%async_computation.4 | async-start | bytes 2621440 | tf_op jit(solution)/shard_map/all_gather | solution.py:148
  320.6 351.2 %copy-start.2 = (f32[8,128,128]{1,2,0:T(8,128)}, f32[8,128,128]{1,2,0:T(8,128)S(1)}, u32[]{:S(2)}) copy-start(f32[8,128,128]{1,2,0:T(8,128)S(1)} %fusion.21) | copy-start | bytes 1572868
  697.4 13.7 %copy-start.1 = (bf16[1024,1024]{1,0:T(8,128)(2,1)S(1)}, bf16[1024,1024]{1,0:T(8,128)(2,1)}, u32[]{:S(2)}) copy-start(bf16[1024,1024]{1,0:T(8,128)(2,1)} %param.18) | copy-start | bytes 6291460
Sparse Core Ops, SparseCore 0:
  10.3 51.9 all-gather.2
Sparse Core Ops, SparseCore 1:
  305.1 23.8 all-gather.4
where the time goes:
time: 721 us; the launch traced here: 719 us
  waiting for transfers between devices  332 us (46%)
  local copies, waits for them, and re-layouts  235 us (33%)
  blocking collectives  62.1 us (9%)
  matrix products  32.6 us (5%)
  other arithmetic  21.9 us (3%)
  starting transfers between devices  18.8 us (3%)
  between operations  15.1 us (2%)
    all_to_all x1, waiting for transfers between devices, body(): lax.all_to_all(values, 'mem', split_axis=0, concat_axis=0, tiled=True)  331 us
    all_gather x2, blocking collectives, combined_all(): pieces = jax.tree.map(lambda part: lax.all_gather(part, axis), value)  62.1 us
    gather x2, local copies, waits for them, and re-layouts, body(): values = memory_values[offsets]  57 us
    gather x1, local copies, waits for them, and re-layouts, body(): memory_keys[offsets]  42.5 us
    reshape x1, local copies, waits for them, and re-layouts, body(): flat_values = values.reshape(shard_count * capacity, head_count, head_size)  25.6 us
    unnamed x20, local copies, waits for them, and re-layouts  24 us
    dynamic_slice x24, local copies, waits for them, and re-layouts, body(): lax.map(score_source, (source_queries, picked_keys, local_rows, source_pe...  21.7 us
    all_to_all x1, local copies, waits for them, and re-layouts, body(): lax.all_to_all(values, 'mem', split_axis=0, concat_axis=0, tiled=True)  18.7 us
  transfers between devices with their start and end apart: 5, of which 1 were waited for; matrix products, arithmetic and copies ran while one was open for 30% of the time, Pallas kernels for 0%

commit v1 on v0

v1 whole, which is shorter than its diff:
```python
import functools

import jax
import jax.numpy as jnp
from jax import lax
from jax.experimental import pallas as pl
from jax.experimental.pallas import tpu as pltpu
from jax.sharding import PartitionSpec as P

LOG2E = 1.4426950408889634
F32 = jnp.float32
BF16 = jnp.bfloat16


def dot(a, b):
    return jnp.dot(a, b, preferred_element_type=F32)


def dot_t(a, b):
    return lax.dot_general(a, b, (((1,), (1,)), ((), ())), preferred_element_type=F32)


def count_block(ids, rows, memory_rows, dtype):
    cols = lax.broadcasted_iota(jnp.int32, (rows, memory_rows), 1)
    total = jnp.zeros((rows, memory_rows), F32)
    for t in range(ids.shape[1]):
        total = total + jnp.where(ids[:, t : t + 1] == cols, 1.0, 0.0)
    return total.astype(dtype)


def shard_kernel(heads, scale, background, ids_ref, q_ref, k_ref, v_ref, n_ref, st_ref, kt_ref):
    memory_rows, width = k_ref.shape
    size = width // heads
    rows = q_ref.shape[0]

    @pl.when(pl.program_id(0) == 0)
    def _():
        for h in range(heads):
            hs = slice(h * size, (h + 1) * size)
            kt_ref[hs, :] = k_ref[:, hs].T

    count = count_block(ids_ref[...], rows, memory_rows, F32)
    lane = lax.broadcasted_iota(jnp.int32, (rows, 128), 1)
    stats = jnp.zeros((rows, 128), F32)
    for h in range(heads):
        hs = slice(h * size, (h + 1) * size)
        s = dot(q_ref[:, hs], kt_ref[hs, :])
        peak = jnp.max(s, axis=1, keepdims=True)
        e = jnp.exp2((s - peak) * (scale * LOG2E))
        w = e * count
        total = jnp.sum(e, axis=1, keepdims=True)
        den = jnp.sum(w, axis=1, keepdims=True)
        n_ref[:, hs] = dot(w.astype(BF16), v_ref[:, hs]).astype(BF16)
        stats = jnp.where(lane == h, peak * scale, stats)
        stats = jnp.where(lane == heads + h, den + background * total, stats)
    st_ref[...] = stats


def final_kernel(heads, scale, q_ref, lk_ref, lv_ref, n_ref, st_ref, gate_ref, ow_ref, out_ref, mixed):
    shards, rows, width = n_ref.shape
    size = width // heads
    causal = lax.broadcasted_iota(jnp.int32, (rows, rows), 0) >= lax.broadcasted_iota(
        jnp.int32, (rows, rows), 1
    )
    for h in range(heads):
        hs = slice(h * size, (h + 1) * size)
        s = dot_t(q_ref[:, hs], lk_ref[:, hs]) * scale
        s = jnp.where(causal, s, -jnp.inf)
        e = jnp.exp(s - jnp.max(s, axis=1, keepdims=True))
        w = (e / jnp.sum(e, axis=1, keepdims=True)).astype(BF16)
        local = dot(w, lv_ref[:, hs])
        peak = st_ref[0, :, h : h + 1]
        for o in range(1, shards):
            peak = jnp.maximum(peak, st_ref[o, :, h : h + 1])
        num = jnp.zeros((rows, size), F32)
        den = jnp.zeros((rows, 1), F32)
        for o in range(shards):
            a = jnp.exp(st_ref[o, :, h : h + 1] - peak)
            num = num + a * n_ref[o, :, hs].astype(F32)
            den = den + a * st_ref[o, :, heads + h : heads + h + 1]
        gate = gate_ref[0:1, h : h + 1]
        mixed[:, hs] = ((gate / den) * num + (1.0 - gate) * local).astype(BF16)
    out_ref[...] = dot(mixed[...], ow_ref[...]).astype(BF16)


def body(queries, local_keys, local_values, memory_keys, memory_values, ids, gate_bias, out_weight):
    shards = lax.axis_size("mem")
    me = lax.axis_index("mem")
    rows, width = queries.shape
    heads = gate_bias.shape[0]
    size = width // heads
    memory_rows = memory_keys.shape[0]
    top = ids.shape[1]
    scale = size**-0.5
    background = top / (memory_rows * shards)
    group_ids = lax.all_gather(ids, "mem", axis=0, tiled=True) - me * memory_rows
    group_queries = lax.all_gather(queries, "mem", axis=0, tiled=True)
    weight = lax.all_gather(out_weight, "pb", axis=0, tiled=True)
    nums, stats = pl.pallas_call(
        functools.partial(shard_kernel, heads, scale, background),
        grid=(shards,),
        out_shape=(
            jax.ShapeDtypeStruct((shards * rows, width), BF16),
            jax.ShapeDtypeStruct((shards * rows, 128), F32),
        ),
        in_specs=[
            pl.BlockSpec((rows, top), lambda i: (i, 0)),
            pl.BlockSpec((rows, width), lambda i: (i, 0)),
            pl.BlockSpec((memory_rows, width), lambda i: (0, 0)),
            pl.BlockSpec((memory_rows, width), lambda i: (0, 0)),
        ],
        out_specs=(
            pl.BlockSpec((rows, width), lambda i: (i, 0)),
            pl.BlockSpec((rows, 128), lambda i: (i, 0)),
        ),
        scratch_shapes=[pltpu.VMEM((width, memory_rows), BF16)],
        compiler_params=pltpu.CompilerParams(vmem_limit_bytes=40 * 1024 * 1024),
        name="shard_attention",
    )(group_ids, group_queries, memory_keys, memory_values)
    nums = lax.all_to_all(nums, "mem", split_axis=0, concat_axis=0, tiled=True)
    stats = lax.all_to_all(stats[:, : 2 * heads], "mem", split_axis=0, concat_axis=0, tiled=True)
    gate = jax.nn.sigmoid(gate_bias)[None, :]
    return pl.pallas_call(
        functools.partial(final_kernel, heads, scale),
        out_shape=jax.ShapeDtypeStruct((rows, width), BF16),
        scratch_shapes=[pltpu.VMEM((rows, width), BF16)],
        compiler_params=pltpu.CompilerParams(vmem_limit_bytes=40 * 1024 * 1024),
        name="combine_and_project",
    )(
        queries,
        local_keys,
        local_values,
        nums.reshape(shards, rows, width),
        stats.reshape(shards, rows, 2 * heads),
        gate,
        weight,
    )


def solution(mesh):
    split = P(("pb", "mem"), None)
    in_specs = (split, split, split, P("mem", None), P("mem", None), split, P(), P("pb", None))
    return jax.shard_map(body, mesh=mesh, in_specs=in_specs, out_specs=split, check_vma=False)
```

time: 721 us -> 186 us (0.26)
  waiting for transfers between devices: 332 us -> 68.6 us
  local copies, waits for them, and re-layouts: 235 us -> 8.86 us
  Pallas kernels: 0 us -> 46 us
  matrix products: 32.6 us -> 0 us
  other arithmetic: 21.9 us -> 0.04 us
  blocking collectives: 62.1 us -> 43.6 us
  starting transfers between devices: 18.8 us -> 3.79 us
    all_to_all x3 -> x1, waiting for transfers between devices: 331 us -> 20.9 us  [body(): nums = lax.all_to_all(nums, 'mem', split_axis=0, concat_axis=0, tiled=True)]
    gather x3 -> x0, local copies, waits for them, and re-layouts: 99.5 us -> none  [the longest x2 57 us: body(): values = memory_values[offsets]]
    pallas_call x0 -> x2, Pallas kernels: none -> 46 us  [the longest x1 41.2 us: body(): pl.pallas_call(functools.partial(shard_kernel, heads, scale, background),...]
    dot_general x15 -> x0, matrix products: 32.6 us -> none  [the longest x8 9.42 us: score_source(): jnp.einsum('qhd,chd->hqc', query_block, key_block, preferred_element_type...]
    scatter x2 -> x0, local copies, waits for them, and re-layouts: 31.8 us -> none  [the longest x1 16.1 us: body(): requests = jnp.full((shard_count * capacity,), -1, jnp.int32).at[slots].s...]
    dynamic_slice x28 -> x0, local copies, waits for them, and re-layouts: 29.3 us -> none  [the longest x24 21.7 us: body(): lax.map(score_source, (source_queries, picked_keys, local_rows, source_pe...]
    all_gather x2 -> x1, blocking collectives: 62.1 us -> 33.5 us  [body(): lax.all_gather(ids, 'mem', axis=0, tiled=True) - me * memory_rows]
    reshape x5 -> x0, local copies, waits for them, and re-layouts: 26.7 us -> none  [the longest x1 25.6 us: body(): flat_values = values.reshape(shard_count * capacity, head_count, head_size)]
  transfers between devices with their start and end apart: 5 -> 3, of which waited for: 1 -> 3; matrix products, arithmetic and copies ran while one was open for 30% -> 1% of each run, Pallas kernels for 0% -> 0%
where the time goes in v1:
time: 186 us
  waiting for transfers between devices  68.6 us (37%)
  Pallas kernels  46 us (25%)
  blocking collectives  43.6 us (23%)
  between operations  14.9 us (8%)
  local copies, waits for them, and re-layouts  8.86 us (5%)
  starting transfers between devices  3.79 us (2%)
    pallas_call x1, Pallas kernels, body(): pl.pallas_call(functools.partial(shard_kernel, heads, scale, background),...  41.2 us
    all_gather x1, blocking collectives, body(): lax.all_gather(ids, 'mem', axis=0, tiled=True) - me * memory_rows  33.5 us
    all_gather x1, waiting for transfers between devices, body(): weight = lax.all_gather(out_weight, 'pb', axis=0, tiled=True)  25 us
    all_gather x1, waiting for transfers between devices, body(): group_queries = lax.all_gather(queries, 'mem', axis=0, tiled=True)  21.5 us
    all_to_all x1, waiting for transfers between devices, body(): nums = lax.all_to_all(nums, 'mem', split_axis=0, concat_axis=0, tiled=True)  20.9 us
    all_to_all x1, blocking collectives, body(): lax.all_to_all(stats[:, :2 * heads], 'mem', split_axis=0, concat_axis=0,...  10.1 us
    unnamed x19, local copies, waits for them, and re-layouts  8.5 us
    pallas_call x1, Pallas kernels, body(): pl.pallas_call(functools.partial(final_kernel, heads, scale), out_shape=j...  4.84 us
  transfers between devices with their start and end apart: 3, of which 3 were waited for; matrix products, arithmetic and copies ran while one was open for 1% of the time, Pallas kernels for 0%

profile of v1, /device:TPU:0, one launch (start us, length us, event | category | flops | bytes accessed | tf_op | source)
XLA Modules:
  0.0 185.8 jit_solution(812197080929607766)
XLA Ops:
  7.4 0.0 all-gather.3.cloned.1.call-start
  7.4 0.7 all-gather.3.cloned.1.call-update
  8.1 0.8 copy.10
  8.9 33.5 %all_gather.9 = s32[1024,32]{1,0:T(8,128)S(1)} all-gather(s32[128,32]{1,0:T(8,128)S(1)} %copy.10), channel_id=1, replica_groups=mesh['mem'=8,'pb'=4] {'mem'}, dimensions={0}, use_global_device_ids=true | all-gather | bytes 147456 | tf_op jit(solution)/shard_map/all_gather | solution.py:96
  42.5 21.5 %all-gather.3.cloned.1.call-done.q_ref = bf16[1024,1024]{1,0:T(8,128)(2,1)} async-done(((bf16[128,1024]{1,0:T(8,128)(2,1)}), bf16[1024,1024]{1,0:T(8,128)(2,1)}) %all-gather.3.cloned.1.call-update) | async-done | bytes 2097168 | tf_op jit(solution)/shard_map/all_gather | solution.py:97
  63.9 1.6 copy-done.1
  65.5 1.6 copy-done.2
  67.1 1.6 copy-done.3
  68.7 41.2 %shard_attention.1 = (bf16[1024,1024]{1,0:T(8,128)(2,1)S(1)}, f32[1024,128]{1,0:T(8,128)S(1)}) custom-call(s32[1024,32]{1,0:T(8,128)S(1)} %broadcast_subtract_fusion.ids_ref, bf16[1024,1024]{1,0:T(8,128)(2,1)S(1)} %copy-done.3, bf16[1024,1024]{1,0:T(8,128)(2,1)S(1)} %copy-done.1, bf16[1024,1024]{1,0:T(8,128)(2,1)S(1)} %copy-done.2), custom_call_target="tpu_custom_call" | custom-call | tf_op jit(solution)/shard_map/shard_attention/pallas_call | solution.py:99
  109.9 0.0 copy-start.4
  109.9 1.3 copy-done.4
  111.2 0.2 copy.11
  111.4 10.1 %all_to_all.18 = f32[8,128,16]{1,2,0:T(8,128)S(1)} all-to-all(f32[8,128,16]{1,2,0:T(8,128)S(1)} %copy.11), channel_id=1, replica_groups=mesh['mem'=8,'pb'=4] {'mem'}, dimensions={0} | all-to-all | bytes 131072 | tf_op jit(solution)/shard_map/all_to_all | solution.py:121
  121.5 3.7 %all-to-all-start = ((bf16[8,128,1024]{2,1,0:T(8,128)(2,1)}), bf16[8,128,1024]{2,1,0:T(8,128)(2,1)S(1)}, u32[]{:S(2)}, u32[]{:S(2)}) async-start(bf16[8,128,1024]{2,1,0:T(8,128)(2,1)} %bitcast.5), calls=%async_computation | async-start | bytes 4194304 | tf_op jit(solution)/shard_map/all_to_all | solution.py:120
  125.2 0.0 all-gather.5.cloned.1.call-start
  125.3 0.5 all-gather.5.cloned.1.call-update
  125.8 0.0 copy-done.8
  125.8 0.2 copy.12.st_ref
  126.0 25.0 %all-gather.5.cloned.1.call-done.ow_ref = bf16[1024,1024]{1,0:T(8,128)(2,1)} async-done(((bf16[256,1024]{1,0:T(8,128)(2,1)}), bf16[1024,1024]{1,0:T(8,128)(2,1)}) %all-gather.5.cloned.1.call-update) | async-done | bytes 2097168 | tf_op jit(solution)/shard_map/all_gather | solution.py:98
  151.1 20.9 %all-to-all-done.n_ref = bf16[8,128,1024]{2,1,0:T(8,128)(2,1)S(1)} async-done(((bf16[8,128,1024]{2,1,0:T(8,128)(2,1)}), bf16[8,128,1024]{2,1,0:T(8,128)(2,1)S(1)}, u32[]{:S(2)}, u32[]{:S(2)}) %all-to-all-start) | async-done | bytes 2097184 | tf_op jit(solution)/shard_map/all_to_all | solution.py:120
  171.9 0.0 copy-done.5
  171.9 0.0 copy-start
  171.9 1.6 copy-done
  173.5 4.8 %combine_and_project.1 = bf16[128,1024]{1,0:T(8,128)(2,1)} custom-call(bf16[128,1024]{1,0:T(8,128)(2,1)S(1)} %copy-done.5, bf16[128,1024]{1,0:T(8,128)(2,1)S(1)} %copy-done.6, bf16[128,1024]{1,0:T(8,128)(2,1)S(1)} %copy-done.7, bf16[8,128,1024]{2,1,0:T(8,128)(2,1)S(1)} %all-to-all-done.n_ref, f32[8,128,16]{2,1,0:T(8,128)S(1)} %copy.12.st_ref, ...), custom_call_target="tpu_custom_call" | custom-call | tf_op jit(solution)/shard_map/combine_and_project/pallas_call | solution.py:123
  (11 shorter events, 0.1 us)
Async XLA Ops:
  7.4 56.6 %all-gather.3.cloned.1.call-start = ((), (), s32[]{:S(2)}) async-start(), calls=%async_computation.2 | async-start | bytes 2359296 | tf_op jit(solution)/shard_map/all_gather | solution.py:97
  63.9 1.6 copy-start.1
  65.5 1.6 copy-start.2
  67.1 1.6 copy-start.3
  109.9 1.3 copy-start.4
  121.5 4.3 %copy-start.8 = (f32[8]{0:T(128)S(1)}, f32[8]{0:T(128)}, u32[]{:S(2)}) copy-start(f32[8]{0:T(128)} %param.14) | copy-start | bytes 100
  121.5 50.5 %copy-start.5 = (bf16[128,1024]{1,0:T(8,128)(2,1)S(1)}, bf16[128,1024]{1,0:T(8,128)(2,1)}, u32[]{:S(2)}) copy-start(bf16[128,1024]{1,0:T(8,128)(2,1)} %q_ref.1) | copy-start | bytes 786436
  121.5 50.5 %copy-start.6 = (bf16[128,1024]{1,0:T(8,128)(2,1)S(1)}, bf16[128,1024]{1,0:T(8,128)(2,1)}, u32[]{:S(2)}) copy-start(bf16[128,1024]{1,0:T(8,128)(2,1)} %lk_ref.1) | copy-start | bytes 786436
  121.5 50.5 %copy-start.7 = (bf16[128,1024]{1,0:T(8,128)(2,1)S(1)}, bf16[128,1024]{1,0:T(8,128)(2,1)}, u32[]{:S(2)}) copy-start(bf16[128,1024]{1,0:T(8,128)(2,1)} %lv_ref.1) | copy-start | bytes 786436
  121.5 50.4 %all-to-all-start = ((bf16[8,128,1024]{2,1,0:T(8,128)(2,1)}), bf16[8,128,1024]{2,1,0:T(8,128)(2,1)S(1)}, u32[]{:S(2)}, u32[]{:S(2)}) async-start(bf16[8,128,1024]{2,1,0:T(8,128)(2,1)} %bitcast.5), calls=%async_computation | async-start | bytes 4194304 | tf_op jit(solution)/shard_map/all_to_all | solution.py:120
  125.2 25.8 %all-gather.5.cloned.1.call-start = ((), (), s32[]{:S(2)}) async-start(), calls=%async_computation.3 | async-start | bytes 2621440 | tf_op jit(solution)/shard_map/all_gather | solution.py:98
  171.9 1.6 copy-start
Sparse Core Ops, SparseCore 0:
  10.3 53.5 all-gather.2
Sparse Core Ops, SparseCore 1:
  127.2 23.7 all-gather.4

commit v2 on v1

v2 whole, which is shorter than its diff:
```python
import functools

import jax
import jax.numpy as jnp
from jax import lax
from jax.experimental import pallas as pl
from jax.experimental.pallas import tpu as pltpu
from jax.sharding import PartitionSpec as P

LOG2E = 1.4426950408889634
F32 = jnp.float32
BF16 = jnp.bfloat16
MESH = pl.DeviceIdType.MESH
LANES = 128
ID_WIDTH = 256


def dot(a, b):
    return jnp.dot(a, b, preferred_element_type=F32)


def dot_t(a, b):
    return lax.dot_general(a, b, (((1,), (1,)), ((), ())), preferred_element_type=F32)


def copy_to(src, dst, send_sem, recv_sem, axis, index):
    return pltpu.make_async_remote_copy(
        src_ref=src,
        dst_ref=dst,
        send_sem=send_sem,
        recv_sem=recv_sem,
        device_id={axis: index},
        device_id_type=MESH,
    )


def count_block(ids, first_row, top, memory_rows, count_ref):
    lines = ids.shape[0]
    group = ID_WIDTH // top
    tiles = memory_rows // LANES
    local = ids - first_row
    high = jnp.right_shift(local, 7)
    low = jnp.bitwise_and(local, LANES - 1)
    place = lax.broadcasted_iota(jnp.int32, (tiles * group, ID_WIDTH), 0)
    entry = lax.broadcasted_iota(jnp.int32, (tiles * group, ID_WIDTH), 1)
    wanted = jnp.where(entry // top == place % group, place // group, -(2**30))
    lane = lax.broadcasted_iota(jnp.int32, (LANES, ID_WIDTH), 0)
    for line in range(lines):
        a = jnp.where(high[line : line + 1, :] == wanted, 1.0, 0.0).astype(BF16)
        b = jnp.where(low[line : line + 1, :] == lane, 1.0, 0.0).astype(BF16)
        c = dot_t(a, b)
        for tile in range(tiles):
            count_ref[line * group : (line + 1) * group, tile * LANES : (tile + 1) * LANES] = c[
                tile * group : (tile + 1) * group, :
            ]


def columns(parts, rows):
    used = sum(part.shape[0] for part in parts)
    if used < LANES:
        parts = parts + [jnp.zeros((LANES - used, rows), F32)]
    return jnp.concatenate(parts, axis=0).T


def kernel(
    shards,
    parts,
    heads,
    top,
    scale,
    background,
    q_ref,
    ids_ref,
    lk_ref,
    lv_ref,
    gate_ref,
    k_hbm,
    v_hbm,
    ow_hbm,
    out_ref,
    k_ref,
    kt_ref,
    v_ref,
    ow_ref,
    qbuf,
    idbuf,
    count_ref,
    nbuf,
    nst,
    rbuf,
    rst,
    cbuf,
    cst,
    fbuf,
    fst,
    local_ref,
    mixed,
    load_sem,
    q_send,
    q_recv,
    i_send,
    i_recv,
    r_send,
    r_recv,
    rs_send,
    rs_recv,
    f_send,
    f_recv,
    fs_send,
    fs_recv,
    ow_send,
    ow_recv,
):
    rows, width = q_ref.shape
    size = width // heads
    memory_rows = k_ref.shape[0]
    groups = shards // 2
    me = lax.axis_index("mem")
    mine = lax.axis_index("pb")
    column = lax.rem(me, 2)
    group = lax.div(me, 2)
    pair = me + 1 - 2 * column

    def peer(step):
        return lax.rem(group + step, groups) * 2 + column

    load_k = pltpu.make_async_copy(k_hbm, k_ref, load_sem.at[0])
    load_v = pltpu.make_async_copy(v_hbm, v_ref, load_sem.at[1])
    load_ow = pltpu.make_async_copy(ow_hbm, ow_ref.at[mine], load_sem.at[2])
    load_k.start()
    load_v.start()
    load_ow.start()
    qbuf[0] = q_ref[...]
    idbuf[0] = ids_ref[...]

    barrier = pltpu.get_barrier_semaphore()
    pl.semaphore_signal(barrier, inc=1, device_id={"mem": pair}, device_id_type=MESH)
    for step in range(1, groups):
        pl.semaphore_signal(barrier, inc=1, device_id={"mem": peer(step)}, device_id_type=MESH)
    for step in range(1, parts):
        pl.semaphore_signal(
            barrier, inc=1, device_id={"pb": lax.rem(mine + step, parts)}, device_id_type=MESH
        )
    pl.semaphore_wait(barrier, 1 + (groups - 1) + (parts - 1))

    def forward(j):
        return (
            copy_to(qbuf.at[2 * j], qbuf.at[2 * j + 1], q_send.at[j], q_recv.at[2 * j + 1], "mem", pair),
            copy_to(idbuf.at[2 * j], idbuf.at[2 * j + 1], i_send.at[j], i_recv.at[2 * j + 1], "mem", pair),
        )

    def spread(j):
        return (
            copy_to(qbuf.at[0], qbuf.at[2 * j], q_send.at[groups + j], q_recv.at[2 * j], "mem", peer(j)),
            copy_to(idbuf.at[0], idbuf.at[2 * j], i_send.at[groups + j], i_recv.at[2 * j], "mem", peer(j)),
        )

    def give(j):
        return (
            copy_to(nbuf.at[2 * j + 1], rbuf.at[j], r_send.at[j], r_recv.at[j], "mem", pair),
            copy_to(nst.at[2 * j + 1], rst.at[j], rs_send.at[j], rs_recv.at[j], "mem", pair),
        )

    def home(j):
        to = peer(groups - j)
        return (
            copy_to(cbuf.at[j], fbuf.at[j], f_send.at[j], f_recv.at[j], "mem", to),
            copy_to(cst.at[j], fst.at[j], fs_send.at[j], fs_recv.at[j], "mem", to),
        )

    def weight(step):
        return copy_to(
            ow_hbm,
            ow_ref.at[mine],
            ow_send.at[step],
            ow_recv.at[step],
            "pb",
            lax.rem(mine + step, parts),
        )

    for copy in forward(0):
        copy.start()
    for step in range(1, groups):
        for copy in spread(step):
            copy.start()
    for step in range(1, parts):
        weight(step).start()

    load_k.wait()
    for h in range(heads):
        hs = slice(h * size, (h + 1) * size)
        kt_ref[hs, :] = k_ref[:, hs].T

    causal = lax.broadcasted_iota(jnp.int32, (rows, rows), 0) >= lax.broadcasted_iota(
        jnp.int32, (rows, rows), 1
    )
    for h in range(heads):
        hs = slice(h * size, (h + 1) * size)
        s = dot_t(q_ref[:, hs], lk_ref[:, hs]) * scale
        s = jnp.where(causal, s, -jnp.inf)
        e = jnp.exp(s - jnp.max(s, axis=1, keepdims=True))
        w = (e / jnp.sum(e, axis=1, keepdims=True)).astype(BF16)
        local_ref[:, hs] = dot(w, lv_ref[:, hs]) * (1.0 - gate_ref[0:1, h : h + 1])
    load_v.wait()

    lane = lax.broadcasted_iota(jnp.int32, (rows, LANES), 1)

    def combine(j):
        for copy in give(j):
            copy.wait_recv()
        own_peak, own_den = nst[2 * j, :heads, :], nst[2 * j, heads:, :]
        got_peak, got_den = rst[j, :heads, :], rst[j, heads:, :]
        peak = jnp.maximum(own_peak, got_peak)
        own, got = jnp.exp(own_peak - peak), jnp.exp(got_peak - peak)
        cst[j, :heads, :] = peak
        cst[j, heads:, :] = own * own_den + got * got_den
        turned = columns([own, got], rows)
        for h in range(heads):
            hs = slice(h * size, (h + 1) * size)
            cbuf[j, :, hs] = (
                turned[:, h : h + 1] * nbuf[2 * j, :, hs].astype(F32)
                + turned[:, heads + h : heads + h + 1] * rbuf[j, :, hs].astype(F32)
            ).astype(BF16)

        @pl.when(j > 0)
        def _():
            for copy in home(j):
                copy.start()

    def step_of(i, carry):
        j = lax.div(i, 2)
        odd = lax.rem(i, 2)

        @pl.when(odd == 1)
        def _():
            for copy in forward(j):
                copy.wait_recv()

            @pl.when(j + 1 < groups)
            def _():
                for copy in spread(j + 1):
                    copy.wait_recv()
                for copy in forward(j + 1):
                    copy.start()

        count_block(idbuf[i], me * memory_rows, top, memory_rows, count_ref)
        stats = jnp.zeros((rows, LANES), F32)
        for h in range(heads):
            hs = slice(h * size, (h + 1) * size)
            s = dot(qbuf[i, :, hs], kt_ref[hs, :])
            peak = jnp.max(s, axis=1, keepdims=True)
            e = jnp.exp2((s - peak) * (scale * LOG2E))
            w = e * count_ref[...]
            total = jnp.sum(e, axis=1, keepdims=True)
            den = jnp.sum(w, axis=1, keepdims=True)
            nbuf[i, :, hs] = dot(w.astype(BF16), v_ref[:, hs]).astype(BF16)
            stats = jnp.where(lane == h, peak * scale, stats)
            stats = jnp.where(lane == heads + h, den + background * total, stats)
        nst[i] = stats.T[: 2 * heads, :]

        @pl.when(odd == 1)
        def _():
            for copy in give(j):
                copy.start()

            @pl.when(j > 0)
            def _():
                combine(j - 1)

        return carry

    lax.fori_loop(0, shards, step_of, 0)
    combine(groups - 1)

    for j in range(1, groups):
        for copy in home(j):
            copy.wait_recv()
    stats = [cst[0]] + [fst[j] for j in range(1, groups)]
    peak = stats[0][:heads, :]
    for st in stats[1:]:
        peak = jnp.maximum(peak, st[:heads, :])
    shares = [jnp.exp(st[:heads, :] - peak) for st in stats]
    den = shares[0] * stats[0][heads:, :]
    for share, st in zip(shares[1:], stats[1:]):
        den = den + share * st[heads:, :]
    turned = []
    per_turn = LANES // heads
    for first in range(0, groups, per_turn):
        turned.append(columns([share / den for share in shares[first : first + per_turn]], rows))
    for h in range(heads):
        hs = slice(h * size, (h + 1) * size)
        num = jnp.zeros((rows, size), F32)
        for j in range(groups):
            block = cbuf[0, :, hs] if j == 0 else fbuf[j, :, hs]
            at = (j % per_turn) * heads + h
            num = num + turned[j // per_turn][:, at : at + 1] * block.astype(F32)
        mixed[:, hs] = (gate_ref[0:1, h : h + 1] * num + local_ref[:, hs]).astype(BF16)

    load_ow.wait()
    for step in range(1, parts):
        weight(step).wait_recv()
    depth = width // parts
    result = dot(mixed[:, :depth], ow_ref[0])
    for part in range(1, parts):
        result = result + dot(mixed[:, part * depth : (part + 1) * depth], ow_ref[part])
    out_ref[...] = result.astype(BF16)

    for j in range(groups):
        for copy in forward(j) + give(j):
            copy.wait_send()
    for j in range(1, groups):
        for copy in spread(j) + home(j):
            copy.wait_send()
    for step in range(1, parts):
        weight(step).wait_send()


def body(queries, local_keys, local_values, memory_keys, memory_values, ids, gate_bias, out_weight):
    shards = lax.axis_size("mem")
    parts = lax.axis_size("pb")
    rows, width = queries.shape
    heads = gate_bias.shape[0]
    memory_rows = memory_keys.shape[0]
    top = ids.shape[1]
    groups = shards // 2
    lines = rows * top // ID_WIDTH
    gate = jax.nn.sigmoid(gate_bias)[None, :]
    vmem = pl.BlockSpec(memory_space=pltpu.VMEM)
    hbm = pl.BlockSpec(memory_space=pl.ANY)
    dma = pltpu.SemaphoreType.DMA
    return pl.pallas_call(
        functools.partial(
            kernel,
            shards,
            parts,
            heads,
            top,
            (width // heads) ** -0.5,
            top / (memory_rows * shards),
        ),
        out_shape=jax.ShapeDtypeStruct((rows, width), BF16),
        in_specs=[vmem] * 5 + [hbm] * 3,
        out_specs=vmem,
        scratch_shapes=[
            pltpu.VMEM((memory_rows, width), BF16),
            pltpu.VMEM((width, memory_rows), BF16),
            pltpu.VMEM((memory_rows, width), BF16),
            pltpu.VMEM((parts, width // parts, width), BF16),
            pltpu.VMEM((shards, rows, width), BF16),
            pltpu.VMEM((shards, lines, ID_WIDTH), jnp.int32),
            pltpu.VMEM((rows, memory_rows), F32),
            pltpu.VMEM((shards, rows, width), BF16),
            pltpu.VMEM((shards, 2 * heads, rows), F32),
            pltpu.VMEM((groups, rows, width), BF16),
            pltpu.VMEM((groups, 2 * heads, rows), F32),
            pltpu.VMEM((groups, rows, width), BF16),
            pltpu.VMEM((groups, 2 * heads, rows), F32),
            pltpu.VMEM((groups, rows, width), BF16),
            pltpu.VMEM((groups, 2 * heads, rows), F32),
            pltpu.VMEM((rows, width), F32),
            pltpu.VMEM((rows, width), BF16),
            dma((3,)),
            dma((shards,)),
            dma((shards,)),
            dma((shards,)),
            dma((shards,)),
            dma((groups,)),
            dma((groups,)),
            dma((groups,)),
            dma((groups,)),
            dma((groups,)),
            dma((groups,)),
            dma((groups,)),
            dma((groups,)),
            dma((parts,)),
            dma((parts,)),
        ],
        compiler_params=pltpu.CompilerParams(
            collective_id=0, has_side_effects=True, vmem_limit_bytes=56 * 1024 * 1024
        ),
        name="retrieval_attention",
    )(
        queries,
        ids.reshape(lines, ID_WIDTH),
        local_keys,
        local_values,
        gate,
        memory_keys,
        memory_values,
        out_weight,
    )


def solution(mesh):
    split = P(("pb", "mem"), None)
    in_specs = (split, split, split, P("mem", None), P("mem", None), split, P(), P("pb", None))
    return jax.shard_map(body, mesh=mesh, in_specs=in_specs, out_specs=split, check_vma=False)
```

time: 186 us -> 79.7 us (0.43)
  waiting for transfers between devices: 68.6 us -> 0 us
  blocking collectives: 43.6 us -> 0 us
  Pallas kernels: 46 us -> 75.1 us
  between operations: 14.9 us -> 0.01 us
  local copies, waits for them, and re-layouts: 8.86 us -> 3.18 us
  starting transfers between devices: 3.79 us -> 0 us
    all_gather x2 -> x0, waiting for transfers between devices: 46.5 us -> none  [the longest x1 25 us: body(): weight = lax.all_gather(out_weight, 'pb', axis=0, tiled=True)]
    all_gather x1 -> x0, blocking collectives: 33.5 us -> none  [body(): lax.all_gather(ids, 'mem', axis=0, tiled=True) - me * memory_rows]
    pallas_call x2 -> x1, Pallas kernels: 46 us -> 75.1 us  [body(): pl.pallas_call(functools.partial(kernel, shards, parts, heads, top, (widt...]
    all_to_all x1 -> x0, waiting for transfers between devices: 20.9 us -> none  [body(): nums = lax.all_to_all(nums, 'mem', split_axis=0, concat_axis=0, tiled=True)]
    all_to_all x1 -> x0, blocking collectives: 10.1 us -> none  [body(): lax.all_to_all(stats[:, :2 * heads], 'mem', split_axis=0, concat_axis=0,...]
    unnamed x19 -> x2, local copies, waits for them, and re-layouts: 8.5 us -> 2.48 us
    all_to_all x1 -> x0, starting transfers between devices: 3.75 us -> none  [body(): nums = lax.all_to_all(nums, 'mem', split_axis=0, concat_axis=0, tiled=True)]
  transfers between devices with their start and end apart: 3 -> 0, of which waited for: 3 -> 0; matrix products, arithmetic and copies ran while one was open for 1% -> 0% of each run, Pallas kernels for 0% -> 0%
where the time goes in v2:
time: 79.7 us; the launch traced here: 79.5 us
  Pallas kernels  75.1 us (94%)
  local copies, waits for them, and re-layouts  3.18 us (4%)
  other arithmetic  1.24 us (2%)
    pallas_call x1, Pallas kernels, body(): pl.pallas_call(functools.partial(kernel, shards, parts, heads, top, (widt...  75.1 us
    unnamed x2, local copies, waits for them, and re-layouts  2.48 us

profile of v2, /device:TPU:0, one launch (start us, length us, event | category | flops | bytes accessed | tf_op | source)
XLA Modules:
  0.0 79.5 jit_solution(17791586572074295912)
XLA Ops:
  0.0 1.2 %divide_bitcast_fusion.gate_ref = f32[1,8]{1,0:T(1,128)} fusion(f32[8]{0:T(128)} %param.14), kind=kLoop, calls=%fused_computation | loop fusion | flops 24 | bytes 64 | tf_op jit(solution)/shard_map/broadcast_in_dim | solution.py:327
  1.2 0.8 %copy.10 = s32[128,32]{1,0:T(8,128)S(1)} copy(s32[128,32]{0,1:T(8,128)} %param.13) | data formatting | bytes 32768 | tf_op args[5]
  2.1 0.7 reshape.3.ids_ref
  2.7 75.1 %retrieval_attention.1 = bf16[128,1024]{1,0:T(8,128)(2,1)} custom-call(bf16[128,1024]{1,0:T(8,128)(2,1)} %q_ref.1, s32[16,256]{1,0:T(8,128)} %reshape.3.ids_ref, bf16[128,1024]{1,0:T(8,128)(2,1)} %lk_ref.1, bf16[128,1024]{1,0:T(8,128)(2,1)} %lv_ref.1, f32[1,8]{1,0:T(1,128)} %divide_bitcast_fusion.gate_ref, bf16[1024,1024]{1,0:T(8,128)(2,1)} %k_hbm.1, ...), custom_call_target="tpu_custom_call" | custom-call | tf_op jit(solution)/shard_map/retrieval_attention/pallas_call | solution.py:331
  77.8 1.7 %copy.12 = bf16[128,1024]{1,0:T(8,128)(2,1)} copy(bf16[128,1024]{1,0:T(8,128)(2,1)} %retrieval_attention.1) | data formatting | bytes 524288

commit v3 on v2

--- a/solution.py
+++ b/solution.py
@@ -124,6 +124,10 @@
     def peer(step):
         return lax.rem(group + step, groups) * 2 + column
 
+    def away(j):
+        up = j % 2
+        return up * ((j + 1) // 2) + (1 - up) * (groups - j // 2)
+
     load_k = pltpu.make_async_copy(k_hbm, k_ref, load_sem.at[0])
     load_v = pltpu.make_async_copy(v_hbm, v_ref, load_sem.at[1])
     load_ow = pltpu.make_async_copy(ow_hbm, ow_ref.at[mine], load_sem.at[2])
@@ -151,8 +155,8 @@
 
     def spread(j):
         return (
-            copy_to(qbuf.at[0], qbuf.at[2 * j], q_send.at[groups + j], q_recv.at[2 * j], "mem", peer(j)),
-            copy_to(idbuf.at[0], idbuf.at[2 * j], i_send.at[groups + j], i_recv.at[2 * j], "mem", peer(j)),
+            copy_to(qbuf.at[0], qbuf.at[2 * j], q_send.at[groups + j], q_recv.at[2 * j], "mem", peer(away(j))),
+            copy_to(idbuf.at[0], idbuf.at[2 * j], i_send.at[groups + j], i_recv.at[2 * j], "mem", peer(away(j))),
         )
 
     def give(j):
@@ -162,7 +166,7 @@
         )
 
     def home(j):
-        to = peer(groups - j)
+        to = peer(groups - away(j))
         return (
             copy_to(cbuf.at[j], fbuf.at[j], f_send.at[j], f_recv.at[j], "mem", to),
             copy_to(cst.at[j], fst.at[j], fs_send.at[j], fs_recv.at[j], "mem", to),
@@ -180,7 +184,7 @@
 
     for copy in forward(0):
         copy.start()
-    for step in range(1, groups):
+    for step in range(1, min(3, groups)):
         for copy in spread(step):
             copy.start()
     for step in range(1, parts):
@@ -202,6 +206,9 @@
         w = (e / jnp.sum(e, axis=1, keepdims=True)).astype(BF16)
         local_ref[:, hs] = dot(w, lv_ref[:, hs]) * (1.0 - gate_ref[0:1, h : h + 1])
     load_v.wait()
+    for step in range(3, groups):
+        for copy in spread(step):
+            copy.start()
 
     lane = lax.broadcasted_iota(jnp.int32, (rows, LANES), 1)
 
@@ -231,17 +238,17 @@
         j = lax.div(i, 2)
         odd = lax.rem(i, 2)
 
+        @pl.when((odd == 0) & (j + 1 < groups))
+        def _():
+            for copy in spread(j + 1):
+                copy.wait_recv()
+            for copy in forward(j + 1):
+                copy.start()
+
         @pl.when(odd == 1)
         def _():
             for copy in forward(j):
                 copy.wait_recv()
-
-            @pl.when(j + 1 < groups)
-            def _():
-                for copy in spread(j + 1):
-                    copy.wait_recv()
-                for copy in forward(j + 1):
-                    copy.start()
 
         count_block(idbuf[i], me * memory_rows, top, memory_rows, count_ref)
         stats = jnp.zeros((rows, LANES), F32)

time: 79.7 us -> 80.2 us (level)
  no operation moved by 1% of the time
where the time goes in v3:
time: 80.2 us; the launch traced here: 79.9 us
  Pallas kernels  75.5 us (94%)
  local copies, waits for them, and re-layouts  3.18 us (4%)
  other arithmetic  1.24 us (2%)
    pallas_call x1, Pallas kernels, body(): pl.pallas_call(functools.partial(kernel, shards, parts, heads, top, (widt...  75.5 us
    unnamed x2, local copies, waits for them, and re-layouts  2.48 us

profile of v3, /device:TPU:0, one launch (start us, length us, event | category | flops | bytes accessed | tf_op | source)
XLA Modules:
  0.0 79.9 jit_solution(6560770236822296393)
XLA Ops:
  0.0 1.2 %divide_bitcast_fusion.gate_ref = f32[1,8]{1,0:T(1,128)} fusion(f32[8]{0:T(128)} %param.14), kind=kLoop, calls=%fused_computation | loop fusion | flops 24 | bytes 64 | tf_op jit(solution)/shard_map/broadcast_in_dim | solution.py:334
  1.2 0.8 %copy.10 = s32[128,32]{1,0:T(8,128)S(1)} copy(s32[128,32]{0,1:T(8,128)} %param.13) | data formatting | bytes 32768 | tf_op args[5]
  2.1 0.7 reshape.3.ids_ref
  2.7 75.5 %retrieval_attention.1 = bf16[128,1024]{1,0:T(8,128)(2,1)} custom-call(bf16[128,1024]{1,0:T(8,128)(2,1)} %q_ref.1, s32[16,256]{1,0:T(8,128)} %reshape.3.ids_ref, bf16[128,1024]{1,0:T(8,128)(2,1)} %lk_ref.1, bf16[128,1024]{1,0:T(8,128)(2,1)} %lv_ref.1, f32[1,8]{1,0:T(1,128)} %divide_bitcast_fusion.gate_ref, bf16[1024,1024]{1,0:T(8,128)(2,1)} %k_hbm.1, ...), custom_call_target="tpu_custom_call" | custom-call | tf_op jit(solution)/shard_map/retrieval_attention/pallas_call | solution.py:338
  78.3 1.7 %copy.12 = bf16[128,1024]{1,0:T(8,128)(2,1)} copy(bf16[128,1024]{1,0:T(8,128)(2,1)} %retrieval_attention.1) | data formatting | bytes 524288

commit v4 on v2

--- a/solution.py
+++ b/solution.py
@@ -187,6 +187,7 @@
         weight(step).start()
 
     load_k.wait()
+    gate = 1.0 / (1.0 + jnp.exp(-gate_ref[...]))
     for h in range(heads):
         hs = slice(h * size, (h + 1) * size)
         kt_ref[hs, :] = k_ref[:, hs].T
@@ -200,7 +201,7 @@
         s = jnp.where(causal, s, -jnp.inf)
         e = jnp.exp(s - jnp.max(s, axis=1, keepdims=True))
         w = (e / jnp.sum(e, axis=1, keepdims=True)).astype(BF16)
-        local_ref[:, hs] = dot(w, lv_ref[:, hs]) * (1.0 - gate_ref[0:1, h : h + 1])
+        local_ref[:, hs] = dot(w, lv_ref[:, hs]) * (1.0 - gate[0:1, h : h + 1])
     load_v.wait()
 
     lane = lax.broadcasted_iota(jnp.int32, (rows, LANES), 1)
@@ -294,7 +295,7 @@
             block = cbuf[0, :, hs] if j == 0 else fbuf[j, :, hs]
             at = (j % per_turn) * heads + h
             num = num + turned[j // per_turn][:, at : at + 1] * block.astype(F32)
-        mixed[:, hs] = (gate_ref[0:1, h : h + 1] * num + local_ref[:, hs]).astype(BF16)
+        mixed[:, hs] = (gate[0:1, h : h + 1] * num + local_ref[:, hs]).astype(BF16)
 
     load_ow.wait()
     for step in range(1, parts):
@@ -324,7 +325,6 @@
     top = ids.shape[1]
     groups = shards // 2
     lines = rows * top // ID_WIDTH
-    gate = jax.nn.sigmoid(gate_bias)[None, :]
     vmem = pl.BlockSpec(memory_space=pltpu.VMEM)
     hbm = pl.BlockSpec(memory_space=pl.ANY)
     dma = pltpu.SemaphoreType.DMA
@@ -384,7 +384,7 @@
         ids.reshape(lines, ID_WIDTH),
         local_keys,
         local_values,
-        gate,
+        gate_bias[None, :],
         memory_keys,
         memory_values,
         out_weight,

time: 79.7 us -> 78.5 us (0.985)
  other arithmetic: 1.24 us -> 0 us
    broadcast_in_dim x1 -> x0, other arithmetic: 1.24 us -> none  [body(): gate = jax.nn.sigmoid(gate_bias)[None, :]]
where the time goes in v4:
time: 78.5 us; the launch traced here: 78.2 us
  Pallas kernels  75.1 us (96%)
  local copies, waits for them, and re-layouts  3.18 us (4%)
    pallas_call x1, Pallas kernels, body(): pl.pallas_call(functools.partial(kernel, shards, parts, heads, top, (widt...  75.1 us
    unnamed x2, local copies, waits for them, and re-layouts  2.48 us

profile of v4, /device:TPU:0, one launch (start us, length us, event | category | flops | bytes accessed | tf_op | source)
XLA Modules:
  0.0 78.2 jit_solution(17446604904832351596)
XLA Ops:
  0.0 0.8 %copy.10 = s32[128,32]{1,0:T(8,128)S(1)} copy(s32[128,32]{0,1:T(8,128)} %param.13) | data formatting | bytes 32768 | tf_op args[5]
  0.8 0.7 reshape.3.ids_ref
  1.5 75.1 %retrieval_attention.1 = bf16[128,1024]{1,0:T(8,128)(2,1)} custom-call(bf16[128,1024]{1,0:T(8,128)(2,1)} %q_ref.1, s32[16,256]{1,0:T(8,128)} %reshape.3.ids_ref, bf16[128,1024]{1,0:T(8,128)(2,1)} %lk_ref.1, bf16[128,1024]{1,0:T(8,128)(2,1)} %lv_ref.1, f32[1,8]{1,0:T(1,128)} %bitcast.1, bf16[1024,1024]{1,0:T(8,128)(2,1)} %k_hbm.1, bf16[1024,1024]{1,0:T(8,128)(2,1)} %v_hbm.1, ...), custom_call_target="tpu_custom_call" | custom-call | tf_op jit(solution)/shard_map/retrieval_attention/pallas_call | solution.py:331
  76.6 1.7 %copy.12 = bf16[128,1024]{1,0:T(8,128)(2,1)} copy(bf16[128,1024]{1,0:T(8,128)(2,1)} %retrieval_attention.1) | data formatting | bytes 524288
